TPU v7x, 32 devices: a whole 2x2x4 slice. The times are simulated.
32 devices in a mesh: section: 4 (over y, x), expert: 8 (over z, core).
Axes of the slice: x: 2, y: 2, z: 4, core: 2. Of those that a mesh axis runs over, the one named last changes fastest.
Arguments:
- inputs: bfloat16 [2, 512, 2048], P(None, 'expert'), may hold values from -45 to 45
- cotangent: bfloat16 [2, 512, 2048], P(None, 'expert'), may hold values from -6 to 6
- lengths: int32 [2, 8], P(None, 'expert'), may hold values from 32 to 64, as said below
- norm_gain: float32 [4, 2048], P('section'), may hold values from 0.1 to 1.9
- router: bfloat16 [4, 2048, 8], P('section'), may hold values from -0.125 to 0.125
- expert_in: bfloat16 [4, 8, 2048, 1536], P('section', 'expert'), may hold values from -0.125 to 0.125
- expert_out: bfloat16 [4, 8, 768, 2048], P('section', 'expert'), may hold values from -0.21875 to 0.21875
- routes: int32 [4, 2, 512, 2], P('section', None, 'expert'), may hold values from 0 to 7, as said below
Outputs:
- section_grads: bfloat16 [4, 2, 512, 2048], P('section', None, 'expert')
- router_grad: float32 [4, 2048, 8], P('section')
- gain_grad: float32 [4, 2048], P('section')
Inputs may be any that keep to these rules, and one draw needn't show every extreme that they name: `lengths`: sequence b of a micro-batch fills positions b * 64 to b * 64 + length - 1; the rest is padding. Each micro-batch has a sequence of length 64. `routes`: each row names 2 different experts. Among the rows of one sequence for one section and micro-batch no expert is named more than 16 times; for each section and micro-batch one expert is named exactly 16 times within the first 32 rows of every sequence. For each section and micro-batch the experts fall into two halves, a row's first choice in one and its second in the other.
All inputs are finite; a program needn't handle non-finite values.
Results may differ from a plain program's by a relative error of at most 0.024.
Values may be sent and summed in bfloat16 or wider, within the bound.
No kernel may reach another device: no remote copies, remote signals or barrier semaphores. Data moves between devices by JAX's collectives and lax.ppermute only.
A program may use at most 128 MiB of HBM per device.

v0:
```python
import jax
import jax.numpy as jnp
from jax import lax
from jax.sharding import PartitionSpec as P

EPSILON = 1e-06


def shifted(block, axis, distance):
    devices = range(lax.axis_size(axis))
    route = [(i - distance, i) for i in devices if i - distance in devices]
    return lax.ppermute(block, axis, route)


def normalize(hidden_in, gain_row):
    values = hidden_in.astype(jnp.float32)
    scale_inv = lax.rsqrt(jnp.mean(values * values, axis=-1, keepdims=True) + EPSILON)
    normed = (values * scale_inv * gain_row).astype(jnp.bfloat16)
    return (values, scale_inv, normed)


def expert_mix(row_block, weight_in):
    return jnp.dot(row_block, weight_in, preferred_element_type=jnp.float32)


def expert_apply(row_block, weight_in, weight_out):
    hidden = weight_out.shape[0]
    mixed_rows = expert_mix(row_block, weight_in)
    gate_part = mixed_rows[:, :hidden]
    up_part = mixed_rows[:, hidden:]
    activated = (gate_part * jax.nn.sigmoid(gate_part) * up_part).astype(jnp.bfloat16)
    result = jnp.dot(activated, weight_out, preferred_element_type=jnp.float32).astype(jnp.bfloat16)
    return (result, mixed_rows)


def expert_adjoint(mixed_rows, grad_rows, weight_in, weight_out):
    hidden = weight_out.shape[0]
    gate_part = mixed_rows[:, :hidden]
    up_part = mixed_rows[:, hidden:]
    act_grad = lax.dot_general(
        grad_rows, weight_out, (((1,), (1,)), ((), ())), preferred_element_type=jnp.float32
    )
    sigmoid_gate = jax.nn.sigmoid(gate_part)
    gate_grad = act_grad * up_part * sigmoid_gate * (1.0 + gate_part * (1.0 - sigmoid_gate))
    up_grad = act_grad * gate_part * sigmoid_gate
    joined = jnp.concatenate([gate_grad, up_grad], axis=1).astype(jnp.bfloat16)
    return lax.dot_general(
        joined, weight_in, (((1,), (1,)), ((), ())), preferred_element_type=jnp.float32
    ).astype(jnp.bfloat16)


def choice_weights(normed, router_local, route_rows):
    experts = router_local.shape[1]
    logits = jnp.dot(normed, router_local, preferred_element_type=jnp.float32)
    expert_codes = lax.broadcasted_iota(jnp.int32, (1, 1, experts), 2)
    chosen = route_rows[:, :, None] == expert_codes
    picked = jnp.sum(jnp.where(chosen, logits[:, None, :], 0.0), axis=-1)
    weights = jax.nn.sigmoid(picked - picked[:, ::-1])
    return (chosen, weights)


def slot_tables(chosen, live_rows, capacity):
    tokens_here, choice_count, experts = chosen.shape
    marked = (
        (chosen & live_rows[:, None, None])
        .reshape(tokens_here * choice_count, experts)
        .astype(jnp.int32)
    )
    earlier = jnp.cumsum(marked, axis=0) - marked
    position = jnp.sum(earlier * marked, axis=1)
    expert_codes = lax.broadcasted_iota(jnp.int32, (1, experts), 1)
    target = jnp.sum(marked * expert_codes, axis=1)
    present = jnp.sum(marked, axis=1) > 0
    slot_of = jnp.where(present, target * capacity + position, -1).reshape(
        tokens_here, choice_count
    )
    slot_codes = lax.broadcasted_iota(jnp.int32, (choice_count, experts * capacity, tokens_here), 1)
    return (jnp.transpose(slot_of)[:, None, :] == slot_codes).astype(jnp.bfloat16)


def store_at(buffer, new_value, slot_index, keep_flag):
    previous = lax.dynamic_index_in_dim(buffer, slot_index, 0, keepdims=False)
    return lax.dynamic_update_index_in_dim(
        buffer, jnp.where(keep_flag, new_value, previous), slot_index, 0
    )


def local(inputs, cotangent, lengths, norm_gain, router, expert_in, expert_out, routes):
    micro_count, tokens_here, model_width = inputs.shape
    sections = lax.axis_size("section")
    section_id = lax.axis_index("section")
    router_local = router[0]
    experts = router_local.shape[1]
    choice_count = routes.shape[3]
    capacity = choice_count * tokens_here // experts
    gain_row = norm_gain[0]
    weight_in = expert_in[0, 0]
    weight_out = expert_out[0, 0]
    hidden = weight_out.shape[0]
    positions = lax.broadcasted_iota(jnp.int32, (micro_count, tokens_here), 1)
    live_all = positions < lengths
    route_all = routes[0]
    ticks = sections + micro_count - 1
    inbox_rows = jnp.zeros((tokens_here, model_width), jnp.bfloat16)
    stored_inputs = jnp.zeros((micro_count, tokens_here, model_width), jnp.bfloat16)
    stored_outputs = jnp.zeros((micro_count, choice_count, tokens_here, model_width), jnp.float32)
    stored_mixed = jnp.zeros((micro_count, experts, capacity, 2 * hidden), jnp.float32)
    for tick_index in range(ticks):
        micro_index = tick_index - section_id
        inside = (micro_index >= 0) & (micro_index < micro_count)
        working = inside
        clipped = jnp.clip(micro_index, 0, micro_count - 1)
        arriving = lax.dynamic_index_in_dim(inputs, clipped, 0, keepdims=False)
        hidden_in = jnp.where(section_id == 0, arriving, inbox_rows)
        values, scale_inv, normed = normalize(hidden_in, gain_row)
        route_rows = lax.dynamic_index_in_dim(route_all, clipped, 0, keepdims=False)
        live_rows = lax.dynamic_index_in_dim(live_all, clipped, 0, keepdims=False)
        chosen, weights = choice_weights(normed, router_local, route_rows)
        pair_table = slot_tables(chosen, live_rows, capacity)
        slot_table = jnp.sum(pair_table, axis=0)
        outgoing = jnp.dot(slot_table, normed, preferred_element_type=jnp.float32).astype(
            jnp.bfloat16
        )
        outgoing = outgoing.reshape(experts, capacity, model_width)
        run_received = lax.all_to_all(outgoing, "expert", split_axis=0, concat_axis=0, tiled=True)
        row_shape = run_received.shape

        def compute(row_block):
            return expert_apply(row_block, weight_in, weight_out)

        def skip_work(row_block):
            return (
                jnp.zeros(row_block.shape, jnp.bfloat16),
                jnp.zeros((row_block.shape[0], 2 * hidden), jnp.float32),
            )

        run_result, mixed_rows = lax.cond(
            working, compute, skip_work, run_received.reshape(-1, model_width)
        )
        returned = lax.all_to_all(
            run_result.reshape(row_shape), "expert", split_axis=0, concat_axis=0, tiled=True
        )
        returned, mixed_rows = (
            returned,
            mixed_rows.reshape(row_shape[0], row_shape[1], 2 * hidden),
        )
        expert_rows = returned.reshape(experts * capacity, model_width)
        per_choice = jnp.einsum(
            "kst,sd->ktd", pair_table, expert_rows, preferred_element_type=jnp.float32
        )
        combined = jnp.sum(jnp.transpose(weights)[:, :, None] * per_choice, axis=0)
        leaving = (values + combined).astype(jnp.bfloat16)
        stored_inputs = store_at(stored_inputs, hidden_in, clipped, inside)
        stored_outputs = store_at(stored_outputs, per_choice, clipped, inside)
        stored_mixed = store_at(stored_mixed, mixed_rows, clipped, inside)
        inbox_rows = shifted(leaving, "section", 1)
    inbox_rows = jnp.zeros((tokens_here, model_width), jnp.bfloat16)
    router_total = jnp.zeros((model_width, experts), jnp.float32)
    gain_total = jnp.zeros((model_width,), jnp.float32)
    grads_out = jnp.zeros((micro_count, tokens_here, model_width), jnp.bfloat16)
    for tick_index in range(ticks):
        micro_index = tick_index - (sections - 1 - section_id)
        inside = (micro_index >= 0) & (micro_index < micro_count)
        working = inside
        clipped = jnp.clip(micro_index, 0, micro_count - 1)
        arriving = lax.dynamic_index_in_dim(cotangent, clipped, 0, keepdims=False)
        grad_in = jnp.where(section_id == sections - 1, arriving, inbox_rows)
        grad_values = grad_in.astype(jnp.float32)
        hidden_in = lax.dynamic_index_in_dim(stored_inputs, clipped, 0, keepdims=False)
        values, scale_inv, normed = normalize(hidden_in, gain_row)
        route_rows = lax.dynamic_index_in_dim(route_all, clipped, 0, keepdims=False)
        live_rows = lax.dynamic_index_in_dim(live_all, clipped, 0, keepdims=False)
        chosen, weights = choice_weights(normed, router_local, route_rows)
        pair_table = slot_tables(chosen, live_rows, capacity)
        per_choice = lax.dynamic_index_in_dim(stored_outputs, clipped, 0, keepdims=False)
        choice_grad = jnp.sum(grad_values[None] * per_choice, axis=-1)
        first_grad = weights[:, 0] * weights[:, 1] * (choice_grad[0] - choice_grad[1])
        pick_grad = jnp.stack([first_grad, -first_grad], axis=1)
        logit_grad = jnp.sum(jnp.where(chosen, pick_grad[:, :, None], 0.0), axis=1).astype(
            jnp.bfloat16
        )
        output_grad = (jnp.transpose(weights)[:, :, None] * grad_values[None]).astype(jnp.bfloat16)
        grad_send = jnp.einsum(
            "kst,ktd->sd", pair_table, output_grad, preferred_element_type=jnp.float32
        )
        grad_send = grad_send.astype(jnp.bfloat16).reshape(experts, capacity, model_width)
        received = lax.all_to_all(grad_send, "expert", split_axis=0, concat_axis=0, tiled=True)
        mixed_flat = lax.dynamic_index_in_dim(stored_mixed, clipped, 0, keepdims=False).reshape(
            -1, 2 * hidden
        )

        def compute_kept(packed):
            return expert_adjoint(packed[0], packed[1], weight_in, weight_out)

        def skip_kept(packed):
            return jnp.zeros(packed[1].shape, jnp.bfloat16)

        result = lax.cond(
            working, compute_kept, skip_kept, (mixed_flat, received.reshape(-1, model_width))
        )
        returned = lax.all_to_all(
            result.reshape(received.shape), "expert", split_axis=0, concat_axis=0, tiled=True
        )
        rows_back = returned.reshape(experts * capacity, model_width)
        normed_grad = jnp.sum(
            jnp.einsum("kst,sd->ktd", pair_table, rows_back, preferred_element_type=jnp.float32),
            axis=0,
        )
        normed_grad = normed_grad + lax.dot_general(
            logit_grad, router_local, (((1,), (1,)), ((), ())), preferred_element_type=jnp.float32
        )
        centred = values * scale_inv
        scaled_grad = normed_grad * gain_row
        input_grad = grad_values + scale_inv * (
            scaled_grad - centred * jnp.mean(scaled_grad * centred, axis=-1, keepdims=True)
        )
        leaving = input_grad.astype(jnp.bfloat16)
        router_piece = lax.dot_general(
            normed, logit_grad, (((0,), (0,)), ((), ())), preferred_element_type=jnp.float32
        )
        router_total = router_total + jnp.where(working, router_piece, 0.0)
        gain_total = gain_total + jnp.where(working, jnp.sum(normed_grad * centred, axis=0), 0.0)
        grads_out = store_at(grads_out, leaving, clipped, inside)
        inbox_rows = shifted(leaving, "section", -1)
    router_sum, gain_sum = lax.psum((router_total, gain_total), "expert")
    denominator = micro_count * choice_count * tokens_here
    return (grads_out[None], (router_sum / denominator)[None], (gain_sum / denominator)[None])


def solution(mesh):
    in_specs = (
        P(None, "expert", None),
        P(None, "expert", None),
        P(None, "expert"),
        P("section", None),
        P("section", None, None),
        P("section", "expert", None, None),
        P("section", "expert", None, None),
        P("section", None, "expert", None),
    )
    out_specs = (P("section", None, "expert", None), P("section", None, None), P("section", None))
    return jax.shard_map(local, mesh=mesh, in_specs=in_specs, out_specs=out_specs, check_vma=False)
```

profile of v0, /device:TPU:0, one launch (start us, length us, event | category | flops | bytes accessed | tf_op | source)
XLA Modules:
  0.0 645.6 jit_solution(7610988853190537436)
XLA Ops:
  26.6 10.0 %all-to-all-done = bf16[8,16,2048]{2,1,0:T(8,128)(2,1)S(1)} async-done(((bf16[8,16,2048]{2,1,0:T(8,128)(2,1)}), bf16[8,16,2048]{2,1,0:T(8,128)(2,1)S(1)}, u32[]{:S(2)}, u32[]{:S(2)}) %all-to-all-start) | async-done | bytes 524320 | tf_op jit(solution)/shard_map/all_to_all | solution.py:125
  48.4 14.4 %all-to-all-done.1 = bf16[8,16,2048]{2,1,0:T(8,128)(2,1)S(1)} async-done(((bf16[8,16,2048]{2,1,0:T(8,128)(2,1)}), bf16[8,16,2048]{2,1,0:T(8,128)(2,1)S(1)}, u32[]{:S(2)}, u32[]{:S(2)}) %all-to-all-start.1) | async-done | bytes 524320 | tf_op jit(solution)/shard_map/all_to_all | solution.py:140
  78.1 13.4 %all-to-all-done.2 = bf16[8,16,2048]{2,1,0:T(8,128)(2,1)S(1)} async-done(((bf16[8,16,2048]{2,1,0:T(8,128)(2,1)}), bf16[8,16,2048]{2,1,0:T(8,128)(2,1)S(1)}, u32[]{:S(2)}, u32[]{:S(2)}) %all-to-all-start.2) | async-done | bytes 524320 | tf_op jit(solution)/shard_map/all_to_all | solution.py:125
  106.1 11.5 %all-to-all-done.3 = bf16[8,16,2048]{2,1,0:T(8,128)(2,1)S(1)} async-done(((bf16[8,16,2048]{2,1,0:T(8,128)(2,1)}), bf16[8,16,2048]{2,1,0:T(8,128)(2,1)S(1)}, u32[]{:S(2)}, u32[]{:S(2)}) %all-to-all-start.3) | async-done | bytes 524320 | tf_op jit(solution)/shard_map/all_to_all | solution.py:140
  137.9 12.5 %all-to-all-done.4 = bf16[8,16,2048]{2,1,0:T(8,128)(2,1)} async-done(((bf16[8,16,2048]{2,1,0:T(8,128)(2,1)}), bf16[8,16,2048]{2,1,0:T(8,128)(2,1)}, u32[]{:S(2)}, u32[]{:S(2)}) %all-to-all-start.4) | async-done | bytes 524320 | tf_op jit(solution)/shard_map/all_to_all | solution.py:125
  159.2 12.7 %all-to-all-done.5 = bf16[8,16,2048]{2,1,0:T(8,128)(2,1)} async-done(((bf16[8,16,2048]{2,1,0:T(8,128)(2,1)}), bf16[8,16,2048]{2,1,0:T(8,128)(2,1)}, u32[]{:S(2)}, u32[]{:S(2)}) %all-to-all-start.5) | async-done | bytes 524320 | tf_op jit(solution)/shard_map/all_to_all | solution.py:140
  174.5 10.1 %collective-permute-start.2 = (bf16[64,2048]{1,0:T(8,128)(2,1)S(1)}, bf16[64,2048]{1,0:T(8,128)(2,1)S(1)}, u32[]{:S(2)}, u32[]{:S(2)}) collective-permute-start(bf16[64,2048]{1,0:T(8,128)(2,1)S(1)} %fusion.170), channel_id=1, source_target_pairs={{0,8},{8,16},{16,24},{1,9},{9,17},{17,25},{2,10},{10,18},{18,26},{... | collective-permute-start | bytes 786440 | tf_op jit(solution)/shard_map/ppermute | solution.py:12
  198.3 13.2 %all-to-all-done.6 = bf16[8,16,2048]{2,1,0:T(8,128)(2,1)} async-done(((bf16[8,16,2048]{2,1,0:T(8,128)(2,1)}), bf16[8,16,2048]{2,1,0:T(8,128)(2,1)}, u32[]{:S(2)}, u32[]{:S(2)}) %all-to-all-start.6) | async-done | bytes 524320 | tf_op jit(solution)/shard_map/all_to_all | solution.py:125
  219.3 12.9 %all-to-all-done.7 = bf16[8,16,2048]{2,1,0:T(8,128)(2,1)S(1)} async-done(((bf16[8,16,2048]{2,1,0:T(8,128)(2,1)}), bf16[8,16,2048]{2,1,0:T(8,128)(2,1)S(1)}, u32[]{:S(2)}, u32[]{:S(2)}) %all-to-all-start.7) | async-done | bytes 524320 | tf_op jit(solution)/shard_map/all_to_all | solution.py:140
  252.2 11.5 %all-to-all-done.9 = bf16[8,16,2048]{2,1,0:T(8,128)(2,1)S(1)} async-done(((bf16[8,16,2048]{2,1,0:T(8,128)(2,1)}), bf16[8,16,2048]{2,1,0:T(8,128)(2,1)S(1)}, u32[]{:S(2)}, u32[]{:S(2)}) %all-to-all-start.9) | async-done | bytes 524320 | tf_op jit(solution)/shard_map/all_to_all | solution.py:125
  292.2 9.8 %all-to-all-done.11 = bf16[8,16,2048]{2,1,0:T(8,128)(2,1)S(1)} async-done(((bf16[8,16,2048]{2,1,0:T(8,128)(2,1)}), bf16[8,16,2048]{2,1,0:T(8,128)(2,1)S(1)}, u32[]{:S(2)}, u32[]{:S(2)}) %all-to-all-start.11) | async-done | bytes 524320 | tf_op jit(solution)/shard_map/all_to_all | solution.py:140
  308.1 13.6 %all-to-all-done.10 = bf16[8,16,2048]{2,1,0:T(8,128)(2,1)} async-done(((bf16[8,16,2048]{2,1,0:T(8,128)(2,1)}), bf16[8,16,2048]{2,1,0:T(8,128)(2,1)}, u32[]{:S(2)}, u32[]{:S(2)}) %all-to-all-start.10) | async-done | bytes 524320 | tf_op jit(solution)/shard_map/all_to_all | solution.py:201
  327.6 14.4 %collective-permute-done.4 = bf16[64,2048]{1,0:T(8,128)(2,1)S(1)} collective-permute-done((bf16[64,2048]{1,0:T(8,128)(2,1)}, bf16[64,2048]{1,0:T(8,128)(2,1)S(1)}, u32[]{:S(2)}, u32[]{:S(2)}) %collective-permute-start.4) | collective-permute-done | bytes 262176 | tf_op jit(solution)/shard_map/ppermute | solution.py:12
  349.1 14.6 %all-to-all-done.12 = bf16[8,16,2048]{2,1,0:T(8,128)(2,1)} async-done(((bf16[8,16,2048]{2,1,0:T(8,128)(2,1)}), bf16[8,16,2048]{2,1,0:T(8,128)(2,1)}, u32[]{:S(2)}, u32[]{:S(2)}) %all-to-all-start.12) | async-done | bytes 524320 | tf_op jit(solution)/shard_map/all_to_all | solution.py:187
  370.2 13.9 %all-to-all-done.13 = bf16[8,16,2048]{2,1,0:T(8,128)(2,1)} async-done(((bf16[8,16,2048]{2,1,0:T(8,128)(2,1)}), bf16[8,16,2048]{2,1,0:T(8,128)(2,1)}, u32[]{:S(2)}, u32[]{:S(2)}) %all-to-all-start.13) | async-done | bytes 524320 | tf_op jit(solution)/shard_map/all_to_all | solution.py:201
  388.4 10.2 %collective-permute-done.5 = bf16[64,2048]{1,0:T(8,128)(2,1)S(1)} collective-permute-done((bf16[64,2048]{1,0:T(8,128)(2,1)}, bf16[64,2048]{1,0:T(8,128)(2,1)S(1)}, u32[]{:S(2)}, u32[]{:S(2)}) %collective-permute-start.5) | collective-permute-done | bytes 262176 | tf_op jit(solution)/shard_map/ppermute | solution.py:12
  406.7 13.7 %all-to-all-done.14 = bf16[8,16,2048]{2,1,0:T(8,128)(2,1)} async-done(((bf16[8,16,2048]{2,1,0:T(8,128)(2,1)}), bf16[8,16,2048]{2,1,0:T(8,128)(2,1)}, u32[]{:S(2)}, u32[]{:S(2)}) %all-to-all-start.14) | async-done | bytes 524320 | tf_op jit(solution)/shard_map/all_to_all | solution.py:187
  426.8 13.9 %all-to-all-done.15 = bf16[8,16,2048]{2,1,0:T(8,128)(2,1)} async-done(((bf16[8,16,2048]{2,1,0:T(8,128)(2,1)}), bf16[8,16,2048]{2,1,0:T(8,128)(2,1)}, u32[]{:S(2)}, u32[]{:S(2)}) %all-to-all-start.15) | async-done | bytes 524320 | tf_op jit(solution)/shard_map/all_to_all | solution.py:201
  445.0 22.6 %collective-permute-done.6 = bf16[64,2048]{1,0:T(8,128)(2,1)S(1)} collective-permute-done((bf16[64,2048]{1,0:T(8,128)(2,1)}, bf16[64,2048]{1,0:T(8,128)(2,1)S(1)}, u32[]{:S(2)}, u32[]{:S(2)}) %collective-permute-start.6) | collective-permute-done | bytes 262176 | tf_op jit(solution)/shard_map/ppermute | solution.py:12
  474.4 14.9 %all-to-all-done.16 = bf16[8,16,2048]{2,1,0:T(8,128)(2,1)} async-done(((bf16[8,16,2048]{2,1,0:T(8,128)(2,1)}), bf16[8,16,2048]{2,1,0:T(8,128)(2,1)}, u32[]{:S(2)}, u32[]{:S(2)}) %all-to-all-start.16) | async-done | bytes 524320 | tf_op jit(solution)/shard_map/all_to_all | solution.py:187
  502.8 14.1 %all-to-all-done.17 = bf16[8,16,2048]{2,1,0:T(8,128)(2,1)} async-done(((bf16[8,16,2048]{2,1,0:T(8,128)(2,1)}), bf16[8,16,2048]{2,1,0:T(8,128)(2,1)}, u32[]{:S(2)}, u32[]{:S(2)}) %all-to-all-start.17) | async-done | bytes 524320 | tf_op jit(solution)/shard_map/all_to_all | solution.py:201
  537.6 13.6 %all-to-all-done.18 = bf16[8,16,2048]{2,1,0:T(8,128)(2,1)} async-done(((bf16[8,16,2048]{2,1,0:T(8,128)(2,1)}), bf16[8,16,2048]{2,1,0:T(8,128)(2,1)}, u32[]{:S(2)}, u32[]{:S(2)}) %all-to-all-start.18) | async-done | bytes 524320 | tf_op jit(solution)/shard_map/all_to_all | solution.py:187
  564.6 54.8 %all-reduce.2.cloned.1.call-done = f32[2048,8]{0,1:T(8,128)} async-done(((f32[2048,8]{0,1:T(8,128)}), f32[2048,8]{0,1:T(8,128)}) %all-reduce.2.cloned.1.call-update) | async-done | bytes 65552 | tf_op jit(solution)/shard_map/psum | solution.py:225
  621.7 14.0 %psum.15 = f32[2048]{0:T(1024)S(1)} all-reduce(f32[2048]{0:T(1024)S(1)} %select_add_fusion), channel_id=1, replica_groups=mesh['section'=4,'expert'=8] {'expert'}, use_global_device_ids=true, to_apply=%region_114.115 | all-reduce | flops 2048 | bytes 16384 | tf_op jit(solution)/shard_map/psum | solution.py:225
  (383 shorter events, 306.3 us)
Async XLA Ops:
  15.0 21.7 %all-to-all-start = ((bf16[8,16,2048]{2,1,0:T(8,128)(2,1)}), bf16[8,16,2048]{2,1,0:T(8,128)(2,1)S(1)}, u32[]{:S(2)}, u32[]{:S(2)}) async-start(bf16[8,16,2048]{2,1,0:T(8,128)(2,1)} %bitcast.31), calls=%async_computation | async-start | bytes 1048576 | tf_op jit(solution)/shard_map/all_to_all | solution.py:125
  44.0 18.8 %all-to-all-start.1 = ((bf16[8,16,2048]{2,1,0:T(8,128)(2,1)}), bf16[8,16,2048]{2,1,0:T(8,128)(2,1)S(1)}, u32[]{:S(2)}, u32[]{:S(2)}) async-start(bf16[8,16,2048]{2,1,0:T(8,128)(2,1)} %bitcast.34), calls=%async_computation.1 | async-start | bytes 1048576 | tf_op jit(solution)/shard_map/all_to_all | solution.py:140
  72.7 18.8 %all-to-all-start.2 = ((bf16[8,16,2048]{2,1,0:T(8,128)(2,1)}), bf16[8,16,2048]{2,1,0:T(8,128)(2,1)S(1)}, u32[]{:S(2)}, u32[]{:S(2)}) async-start(bf16[8,16,2048]{2,1,0:T(8,128)(2,1)} %bitcast.44), calls=%async_computation.2 | async-start | bytes 1048576 | tf_op jit(solution)/shard_map/all_to_all | solution.py:125
  98.9 18.8 %all-to-all-start.3 = ((bf16[8,16,2048]{2,1,0:T(8,128)(2,1)}), bf16[8,16,2048]{2,1,0:T(8,128)(2,1)S(1)}, u32[]{:S(2)}, u32[]{:S(2)}) async-start(bf16[8,16,2048]{2,1,0:T(8,128)(2,1)} %bitcast.45), calls=%async_computation.3 | async-start | bytes 1048576 | tf_op jit(solution)/shard_map/all_to_all | solution.py:140
  130.9 19.5 %all-to-all-start.4 = ((bf16[8,16,2048]{2,1,0:T(8,128)(2,1)}), bf16[8,16,2048]{2,1,0:T(8,128)(2,1)}, u32[]{:S(2)}, u32[]{:S(2)}) async-start(bf16[8,16,2048]{2,1,0:T(8,128)(2,1)} %bitcast.634), calls=%async_computation.4 | async-start | bytes 1048576 | tf_op jit(solution)/shard_map/all_to_all | solution.py:125
  152.4 19.5 %all-to-all-start.5 = ((bf16[8,16,2048]{2,1,0:T(8,128)(2,1)}), bf16[8,16,2048]{2,1,0:T(8,128)(2,1)}, u32[]{:S(2)}, u32[]{:S(2)}) async-start(bf16[8,16,2048]{2,1,0:T(8,128)(2,1)} %bitcast.636), calls=%async_computation.5 | async-start | bytes 1048576 | tf_op jit(solution)/shard_map/all_to_all | solution.py:140
  174.5 15.5 %collective-permute-start.2 = (bf16[64,2048]{1,0:T(8,128)(2,1)S(1)}, bf16[64,2048]{1,0:T(8,128)(2,1)S(1)}, u32[]{:S(2)}, u32[]{:S(2)}) collective-permute-start(bf16[64,2048]{1,0:T(8,128)(2,1)S(1)} %fusion.170), channel_id=1, source_target_pairs={{0,8},{8,16},{16,24},{1,9},{9,17},{17,25},{2,10},{10,18},{18,26},{... | collective-permute-start | bytes 786440 | tf_op jit(solution)/shard_map/ppermute | solution.py:12
  192.0 19.5 %all-to-all-start.6 = ((bf16[8,16,2048]{2,1,0:T(8,128)(2,1)}), bf16[8,16,2048]{2,1,0:T(8,128)(2,1)}, u32[]{:S(2)}, u32[]{:S(2)}) async-start(bf16[8,16,2048]{2,1,0:T(8,128)(2,1)} %bitcast.635), calls=%async_computation.6 | async-start | bytes 1048576 | tf_op jit(solution)/shard_map/all_to_all | solution.py:125
  213.4 18.8 %all-to-all-start.7 = ((bf16[8,16,2048]{2,1,0:T(8,128)(2,1)}), bf16[8,16,2048]{2,1,0:T(8,128)(2,1)S(1)}, u32[]{:S(2)}, u32[]{:S(2)}) async-start(bf16[8,16,2048]{2,1,0:T(8,128)(2,1)} %bitcast.637), calls=%async_computation.7 | async-start | bytes 1048576 | tf_op jit(solution)/shard_map/all_to_all | solution.py:140
  244.8 18.9 %all-to-all-start.9 = ((bf16[8,16,2048]{2,1,0:T(8,128)(2,1)}), bf16[8,16,2048]{2,1,0:T(8,128)(2,1)S(1)}, u32[]{:S(2)}, u32[]{:S(2)}) async-start(bf16[8,16,2048]{2,1,0:T(8,128)(2,1)} %bitcast.633), calls=%async_computation.9 | async-start | bytes 1048576 | tf_op jit(solution)/shard_map/all_to_all | solution.py:125
  263.7 19.5 %all-to-all-start.8 = ((bf16[8,16,2048]{2,1,0:T(8,128)(2,1)}), bf16[8,16,2048]{2,1,0:T(8,128)(2,1)}, u32[]{:S(2)}, u32[]{:S(2)}) async-start(bf16[8,16,2048]{2,1,0:T(8,128)(2,1)} %bitcast.629), calls=%async_computation.8 | async-start | bytes 1048576 | tf_op jit(solution)/shard_map/all_to_all | solution.py:187
  283.2 18.8 %all-to-all-start.11 = ((bf16[8,16,2048]{2,1,0:T(8,128)(2,1)}), bf16[8,16,2048]{2,1,0:T(8,128)(2,1)S(1)}, u32[]{:S(2)}, u32[]{:S(2)}) async-start(bf16[8,16,2048]{2,1,0:T(8,128)(2,1)} %bitcast.94), calls=%async_computation.11 | async-start | bytes 1048576 | tf_op jit(solution)/shard_map/all_to_all | solution.py:140
  302.0 19.7 %all-to-all-start.10 = ((bf16[8,16,2048]{2,1,0:T(8,128)(2,1)}), bf16[8,16,2048]{2,1,0:T(8,128)(2,1)}, u32[]{:S(2)}, u32[]{:S(2)}) async-start(bf16[8,16,2048]{2,1,0:T(8,128)(2,1)} %bitcast.84), calls=%async_computation.10 | async-start | bytes 1048576 | tf_op jit(solution)/shard_map/all_to_all | solution.py:201
  326.0 16.0 %collective-permute-start.4 = (bf16[64,2048]{1,0:T(8,128)(2,1)}, bf16[64,2048]{1,0:T(8,128)(2,1)S(1)}, u32[]{:S(2)}, u32[]{:S(2)}) collective-permute-start(bf16[64,2048]{1,0:T(8,128)(2,1)} %get-tuple-element.297), channel_id=1, source_target_pairs={{8,0},{16,8},{24,16},{9,1},{17,9},{25,17},{10,2},{18,10},{26,18},{... | collective-permute-start | bytes 786440 | tf_op jit(solution)/shard_map/ppermute | solution.py:12
  344.2 19.5 %all-to-all-start.12 = ((bf16[8,16,2048]{2,1,0:T(8,128)(2,1)}), bf16[8,16,2048]{2,1,0:T(8,128)(2,1)}, u32[]{:S(2)}, u32[]{:S(2)}) async-start(bf16[8,16,2048]{2,1,0:T(8,128)(2,1)} %bitcast.632), calls=%async_computation.12 | async-start | bytes 1048576 | tf_op jit(solution)/shard_map/all_to_all | solution.py:187
  364.6 19.5 %all-to-all-start.13 = ((bf16[8,16,2048]{2,1,0:T(8,128)(2,1)}), bf16[8,16,2048]{2,1,0:T(8,128)(2,1)}, u32[]{:S(2)}, u32[]{:S(2)}) async-start(bf16[8,16,2048]{2,1,0:T(8,128)(2,1)} %bitcast.638), calls=%async_computation.13 | async-start | bytes 1048576 | tf_op jit(solution)/shard_map/all_to_all | solution.py:201
  400.8 19.5 %all-to-all-start.14 = ((bf16[8,16,2048]{2,1,0:T(8,128)(2,1)}), bf16[8,16,2048]{2,1,0:T(8,128)(2,1)}, u32[]{:S(2)}, u32[]{:S(2)}) async-start(bf16[8,16,2048]{2,1,0:T(8,128)(2,1)} %bitcast.628), calls=%async_computation.14 | async-start | bytes 1048576 | tf_op jit(solution)/shard_map/all_to_all | solution.py:187
  421.2 19.5 %all-to-all-start.15 = ((bf16[8,16,2048]{2,1,0:T(8,128)(2,1)}), bf16[8,16,2048]{2,1,0:T(8,128)(2,1)}, u32[]{:S(2)}, u32[]{:S(2)}) async-start(bf16[8,16,2048]{2,1,0:T(8,128)(2,1)} %bitcast.639), calls=%async_computation.15 | async-start | bytes 1048576 | tf_op jit(solution)/shard_map/all_to_all | solution.py:201
  443.6 23.9 %collective-permute-start.6 = (bf16[64,2048]{1,0:T(8,128)(2,1)}, bf16[64,2048]{1,0:T(8,128)(2,1)S(1)}, u32[]{:S(2)}, u32[]{:S(2)}) collective-permute-start(bf16[64,2048]{1,0:T(8,128)(2,1)} %get-tuple-element.289), channel_id=1, source_target_pairs={{8,0},{16,8},{24,16},{9,1},{17,9},{25,17},{10,2},{18,10},{26,18},{... | collective-permute-start | bytes 786440 | tf_op jit(solution)/shard_map/ppermute | solution.py:12
  469.8 19.5 %all-to-all-start.16 = ((bf16[8,16,2048]{2,1,0:T(8,128)(2,1)}), bf16[8,16,2048]{2,1,0:T(8,128)(2,1)}, u32[]{:S(2)}, u32[]{:S(2)}) async-start(bf16[8,16,2048]{2,1,0:T(8,128)(2,1)} %bitcast.630), calls=%async_computation.16 | async-start | bytes 1048576 | tf_op jit(solution)/shard_map/all_to_all | solution.py:187
  497.4 19.5 %all-to-all-start.17 = ((bf16[8,16,2048]{2,1,0:T(8,128)(2,1)}), bf16[8,16,2048]{2,1,0:T(8,128)(2,1)}, u32[]{:S(2)}, u32[]{:S(2)}) async-start(bf16[8,16,2048]{2,1,0:T(8,128)(2,1)} %bitcast.640), calls=%async_computation.17 | async-start | bytes 1048576 | tf_op jit(solution)/shard_map/all_to_all | solution.py:201
  531.7 19.5 %all-to-all-start.18 = ((bf16[8,16,2048]{2,1,0:T(8,128)(2,1)}), bf16[8,16,2048]{2,1,0:T(8,128)(2,1)}, u32[]{:S(2)}, u32[]{:S(2)}) async-start(bf16[8,16,2048]{2,1,0:T(8,128)(2,1)} %bitcast.631), calls=%async_computation.18 | async-start | bytes 1048576 | tf_op jit(solution)/shard_map/all_to_all | solution.py:187
  559.1 61.8 %all-to-all-start.19 = ((bf16[8,16,2048]{2,1,0:T(8,128)(2,1)}), bf16[8,16,2048]{2,1,0:T(8,128)(2,1)S(1)}, u32[]{:S(2)}, u32[]{:S(2)}) async-start(bf16[8,16,2048]{2,1,0:T(8,128)(2,1)} %bitcast.160), calls=%async_computation.19 | async-start | bytes 1048576 | tf_op jit(solution)/shard_map/all_to_all | solution.py:201
  562.6 56.8 %all-reduce.2.cloned.1.call-start = ((), (), s32[]{:S(2)}) async-start(), calls=%async_computation.20 | async-start | bytes 131072 | tf_op jit(solution)/shard_map/psum | solution.py:225
  (35 other events, 461.4 us)
Sparse Core Ops, SparseCore 0:
  566.3 53.0 all-reduce.1
where the time goes:
time: 657 us; the launch traced here: 646 us
  waiting for transfers between devices  369 us (56%)
  starting transfers between devices  106 us (16%)
  matrix products  63.2 us (10%)
  other arithmetic  42.5 us (6%)
  local copies, waits for them, and re-layouts  34.9 us (5%)
  between operations  15.7 us (2%)
  blocking collectives  14 us (2%)
    ppermute x8, waiting for transfers between devices, shifted(): return lax.ppermute(block, axis, route)  73.2 us
    all_to_all x5, waiting for transfers between devices, local(): lax.all_to_all(grad_send, 'expert', split_axis=0, concat_axis=0, tiled=True)  63 us
    all_to_all x5, waiting for transfers between devices, local(): lax.all_to_all(run_result.reshape(row_shape), 'expert', split_axis=0, con...  61.3 us
    all_to_all x5, waiting for transfers between devices, local(): lax.all_to_all(outgoing, 'expert', split_axis=0, concat_axis=0, tiled=True)  60.7 us
    all_to_all x5, waiting for transfers between devices, local(): lax.all_to_all(result.reshape(received.shape), 'expert', split_axis=0, co...  55.6 us
    psum x1, waiting for transfers between devices, local(): router_sum, gain_sum = lax.psum((router_total, gain_total), 'expert')  54.8 us
    dynamic_update_slice x19, other arithmetic, store_at(): lax.dynamic_update_index_in_dim(buffer, jnp.where(keep_flag, new_value, p...  25.7 us
    ppermute x8, starting transfers between devices, shifted(): return lax.ppermute(block, axis, route)  25.5 us
  transfers between devices with their start and end apart: 29, of which 28 were waited for; matrix products, arithmetic and copies ran while one was open for 9% of the time, Pallas kernels for 0%

commit v1 on v0

v1 whole, which is shorter than its diff:
```python
import jax
import jax.numpy as jnp
from jax import lax
from jax.sharding import PartitionSpec as P

EPSILON = 1e-06
EXTRA = 128
F32 = jnp.float32
BF16 = jnp.bfloat16


def normalize(hidden_in, gain_row):
    values = hidden_in.astype(F32)
    scale_inv = lax.rsqrt(jnp.mean(values * values, axis=-1, keepdims=True) + EPSILON)
    normed = (values * scale_inv * gain_row).astype(BF16)
    return (values, scale_inv, normed)


def dot(a, b):
    return jnp.dot(a, b, preferred_element_type=F32)


def dot_t(a, b):
    return lax.dot_general(a, b, (((1,), (1,)), ((), ())), preferred_element_type=F32)


def activate(mixed):
    hidden = mixed.shape[1] // 2
    gate, up = (mixed[:, :hidden], mixed[:, hidden:])
    return (gate * jax.nn.sigmoid(gate) * up).astype(BF16)


def adjoint(mixed, grad_rows, weight_in, weight_out):
    hidden = mixed.shape[1] // 2
    gate, up = (mixed[:, :hidden], mixed[:, hidden:])
    act_grad = dot_t(grad_rows, weight_out)
    s = jax.nn.sigmoid(gate)
    gate_grad = act_grad * up * s * (1.0 + gate * (1.0 - s))
    up_grad = act_grad * gate * s
    joined = jnp.concatenate([gate_grad, up_grad], axis=1).astype(BF16)
    choice_grad = jnp.sum(act_grad * (gate * s * up), axis=1, keepdims=True)
    return (dot_t(joined, weight_in).astype(BF16), choice_grad)


def split_pair(column):
    high = column.astype(BF16)
    low = (column - high.astype(F32)).astype(BF16)
    pad = jnp.zeros((column.shape[0], EXTRA - 2), BF16)
    return jnp.concatenate([high, low, pad], axis=1)


def use_permutes(count):
    return count <= 8 and count & (count - 1) == 0


def exchange(rows, count):
    if not use_permutes(count):
        shape = (count, rows.shape[0] // count, rows.shape[1])
        return lax.all_to_all(rows.reshape(shape), "expert", 0, 0, tiled=True).reshape(rows.shape)
    size = rows.shape[0] // count
    got = [None] * count
    got[0] = rows[:size]
    for x in sorted(range(1, count), reverse=True):
        block = rows[x * size : (x + 1) * size]
        got[x] = lax.ppermute(block, "expert", [(i, i ^ x) for i in range(count)])
    return jnp.concatenate(got, axis=0)


def pair_tables(routes, live, experts, capacity, my_index):
    micros, tokens, choices = routes.shape
    codes = lax.broadcasted_iota(jnp.int32, (1, 1, 1, experts), 3)
    chosen = routes[..., None] == codes
    marked = (chosen & live[:, :, None, None]).reshape(micros, tokens * choices, experts)
    marked = marked.astype(jnp.int32)
    earlier = jnp.cumsum(marked, axis=1) - marked
    position = jnp.sum(earlier * marked, axis=2)
    present = jnp.sum(marked, axis=2) > 0
    target = routes.reshape(micros, tokens * choices)
    if use_permutes(experts):
        target = target ^ my_index
    slot_of = jnp.where(present, target * capacity + position, -1)
    slot_of = jnp.transpose(slot_of.reshape(micros, tokens, choices), (0, 2, 1))
    slots = lax.broadcasted_iota(jnp.int32, (1, 1, experts * capacity, 1), 2)
    return (chosen, (slot_of[:, :, None, :] == slots).astype(BF16))


def local(inputs, cotangent, lengths, norm_gain, router, expert_in, expert_out, routes):
    micros, tokens, width = inputs.shape
    sections = lax.axis_size("section")
    section = lax.axis_index("section")
    router_local = router[0]
    experts = router_local.shape[1]
    choices = routes.shape[3]
    capacity = choices * tokens // experts
    gain_row = norm_gain[0]
    weight_in, weight_out = (expert_in[0, 0], expert_out[0, 0])
    last = sections - 1
    ticks = 2 * sections
    assert micros == 2 and choices == 2 and sections >= 3
    positions = lax.broadcasted_iota(jnp.int32, (micros, tokens), 1)
    chosen, tables = pair_tables(
        routes[0], positions < lengths, experts, capacity, lax.axis_index("expert")
    )
    is_last = section == last

    def first_at(tick):
        return tick if tick <= last else 2 * last - tick

    def pick(tick, pair):
        if tick == 0:
            return pair[0]
        if tick == ticks - 1:
            return pair[1]
        return jnp.where(section == first_at(tick), pair[0], pair[1])

    def kept(tick, store):
        early, late = (2 * last - tick, 2 * last + 2 - tick)
        if early not in store or late not in store:
            return store[early] if early in store else store[late]
        return jnp.where(section == early, store[early], store[late])

    hiddens, mixes, rows_home, weights_at, cot_rows = ({}, {}, {}, {}, {})
    inbox = None
    grads = [None, None]
    router_total = jnp.zeros((experts, width), F32)
    gain_total = jnp.zeros((width,), F32)
    for tick in range(ticks):
        forward = tick <= sections
        backward = tick >= last
        both = forward and backward
        table = pick(tick, tables)
        chosen_now = pick(tick, chosen)
        slot_table = jnp.sum(table, axis=0)
        if forward:
            hidden = inbox
            if tick < micros:
                hidden = inputs[tick] if tick == 0 else jnp.where(section == 0, inputs[tick], inbox)
            values, scale_inv, normed = normalize(hidden, gain_row)
            hiddens[tick] = hidden
            source = normed
            if tick < micros:
                source = jnp.where(is_last, cotangent[tick], normed)
        if backward:
            grad = inbox
            if both:
                grad = jnp.where(is_last, cotangent[tick - last], inbox)
            if tick > last:
                source = jnp.where(is_last, normed, grad) if both else grad
        outgoing = dot(slot_table, source).astype(BF16)
        received = exchange(outgoing, experts)
        if tick < micros:
            cot_rows[tick] = received

        if forward:
            logits = dot(normed, router_local)
            picked = jnp.sum(jnp.where(chosen_now, logits[:, None, :], 0.0), axis=-1)
            weights_at[tick] = jax.nn.sigmoid(picked - picked[:, ::-1])

        if not backward:
            mixes[tick] = dot(received, weight_in)
            result = dot(activate(mixes[tick]), weight_out).astype(BF16)
        elif tick == last:

            def visit_once(packed):
                rows, grad_rows = packed
                mixed = dot(rows, weight_in)
                back, choice_grad = adjoint(mixed, grad_rows, weight_in, weight_out)
                return (back, split_pair(choice_grad), mixed)

            def visit_forward(packed):
                mixed = dot(packed[0], weight_in)
                out = dot(activate(mixed), weight_out).astype(BF16)
                return (out, jnp.zeros((out.shape[0], EXTRA), BF16), mixed)

            result, extra, mixes[tick] = lax.cond(
                is_last, visit_once, visit_forward, (received, cot_rows[0])
            )
            result = jnp.concatenate([result, extra], axis=1)
        elif both:
            mixed = lax.cond(
                is_last, lambda rows: dot(rows, weight_in), lambda rows: mixes[last - 1], received
            )
            grad_rows = jnp.where(is_last, cot_rows[1], received)
            result, choice_grad = adjoint(mixed, grad_rows, weight_in, weight_out)
            result = jnp.concatenate([result, split_pair(choice_grad)], axis=1)
        else:
            result = adjoint(kept(tick, mixes), received, weight_in, weight_out)[0]
        returned = exchange(result, experts)
        per_choice = jnp.einsum("kst,sd->ktd", table, returned, preferred_element_type=F32)
        extra_back = per_choice[:, :, width:]
        per_choice = per_choice[:, :, :width]

        if forward:
            rows_home[tick] = returned[:, :width]
            weights = jnp.transpose(weights_at[tick])[:, :, None]
            leaving = (values + jnp.sum(weights * per_choice, axis=0)).astype(BF16)
        if backward:
            values, scale_inv, normed = normalize(kept(tick, hiddens), gain_row)
            weights = kept(tick, weights_at)
            grad_values = grad.astype(F32)
            if both:
                choice_grad = extra_back[:, :, 0] + extra_back[:, :, 1]
            if tick > last:
                outputs = kept(tick, {k: v for k, v in rows_home.items() if k < sections})
                outputs = jnp.einsum("kst,sd->ktd", table, outputs, preferred_element_type=F32)
                stored_grad = jnp.sum(grad_values[None] * outputs, axis=-1)
                choice_grad = jnp.where(is_last, choice_grad, stored_grad) if both else stored_grad
            first_grad = weights[:, 0] * weights[:, 1] * (choice_grad[0] - choice_grad[1])
            pick_grad = jnp.stack([first_grad, -first_grad], axis=1)
            logit_grad = jnp.sum(jnp.where(chosen_now, pick_grad[:, :, None], 0.0), axis=1)
            logit_grad = logit_grad.astype(BF16)
            normed_grad = jnp.sum(jnp.transpose(weights)[:, :, None] * per_choice, axis=0)
            normed_grad = normed_grad + dot_t(logit_grad, router_local)
            centred = values * scale_inv
            scaled_grad = normed_grad * gain_row
            input_grad = grad_values + scale_inv * (
                scaled_grad - centred * jnp.mean(scaled_grad * centred, axis=-1, keepdims=True)
            )
            input_grad = input_grad.astype(BF16)
            active = (section == 2 * last - tick) | (section == 2 * last + 1 - tick)
            router_piece = lax.dot_general(
                logit_grad, normed, (((0,), (0,)), ((), ())), preferred_element_type=F32
            )
            router_total = router_total + jnp.where(active, router_piece, 0.0)
            gain_total = gain_total + jnp.where(active, jnp.sum(normed_grad * centred, axis=0), 0.0)
            leaving = jnp.where(is_last, input_grad, leaving) if tick == last else input_grad
            for micro in range(micros):
                here = section == 2 * last + micro - tick
                if grads[micro] is None:
                    grads[micro] = input_grad
                else:
                    grads[micro] = jnp.where(here, input_grad, grads[micro])
        if tick < ticks - 1:
            route = []
            for micro in range(micros):
                step = tick - micro
                if 0 <= step < 2 * last:
                    route.append((first_at(step), first_at(step + 1)))
            inbox = lax.ppermute(leaving, "section", route)
    router_sum = lax.psum(router_total, "expert")
    gain_sum = lax.psum(gain_total, "expert")
    denominator = micros * choices * tokens
    return (
        jnp.stack(grads)[None],
        jnp.transpose(router_sum / denominator)[None],
        (gain_sum / denominator)[None],
    )


def solution(mesh):
    in_specs = (
        P(None, "expert", None),
        P(None, "expert", None),
        P(None, "expert"),
        P("section", None),
        P("section", None, None),
        P("section", "expert", None, None),
        P("section", "expert", None, None),
        P("section", None, "expert", None),
    )
    out_specs = (P("section", None, "expert", None), P("section", None, None), P("section", None))
    return jax.shard_map(local, mesh=mesh, in_specs=in_specs, out_specs=out_specs, check_vma=False)
```

time: 657 us -> 499 us (0.76)
  waiting for transfers between devices: 369 us -> 179 us
  starting transfers between devices: 106 us -> 165 us
  other arithmetic: 42.5 us -> 22 us
    all_to_all x20 -> x0, waiting for transfers between devices: 241 us -> none  [the longest x5 63 us: local(): lax.all_to_all(grad_send, 'expert', split_axis=0, concat_axis=0, tiled=True)]
    ppermute x8 -> x119, starting transfers between devices: 25.5 us -> 165 us  [the longest x112 151 us: exchange(): got[x] = lax.ppermute(block, 'expert', [(i, i ^ x) for i in range(count)])]
    all_to_all x20 -> x0, starting transfers between devices: 80.9 us -> none  [the longest x5 21.7 us: local(): lax.all_to_all(outgoing, 'expert', split_axis=0, concat_axis=0, tiled=True)]
    ppermute x8 -> x119, waiting for transfers between devices: 73.2 us -> 147 us  [the longest x112 84.9 us: exchange(): got[x] = lax.ppermute(block, 'expert', [(i, i ^ x) for i in range(count)])]
    dynamic_update_slice x19 -> x0, other arithmetic: 25.7 us -> none  [store_at(): lax.dynamic_update_index_in_dim(buffer, jnp.where(keep_flag, new_value, p...]
    psum x1, waiting for transfers between devices: 54.8 us -> 32.1 us  [local(): router_sum = lax.psum(router_total, 'expert')]
    unnamed x53 -> x237, local copies, waits for them, and re-layouts: 4.88 us -> 20.3 us
    dynamic_slice x24 -> x0, local copies, waits for them, and re-layouts: 14.5 us -> none  [the longest x11 9.96 us: store_at(): previous = lax.dynamic_index_in_dim(buffer, slot_index, 0, keepdims=False)]
  transfers between devices with their start and end apart: 29 -> 120, of which waited for: 28 -> 21; matrix products, arithmetic and copies ran while one was open for 9% -> 8% of each run, Pallas kernels for 0% -> 0%
where the time goes in v1:
time: 499 us; the launch traced here: 492 us
  waiting for transfers between devices  179 us (36%)
  starting transfers between devices  165 us (33%)
  matrix products  62.1 us (12%)
  local copies, waits for them, and re-layouts  31.5 us (6%)
  other arithmetic  22 us (4%)
  between operations  16.7 us (3%)
  blocking collectives  15.8 us (3%)
    ppermute x112, starting transfers between devices, exchange(): got[x] = lax.ppermute(block, 'expert', [(i, i ^ x) for i in range(count)])  151 us
    ppermute x112, waiting for transfers between devices, exchange(): got[x] = lax.ppermute(block, 'expert', [(i, i ^ x) for i in range(count)])  84.9 us
    ppermute x7, waiting for transfers between devices, local(): inbox = lax.ppermute(leaving, 'section', route)  62.2 us
    psum x1, waiting for transfers between devices, local(): router_sum = lax.psum(router_total, 'expert')  32.1 us
    dot_general x13, matrix products, dot_t(): lax.dot_general(a, b, (((1,), (1,)), ((), ())), preferred_element_type=F32)  29.5 us
    dot_general x21, matrix products, dot(): return jnp.dot(a, b, preferred_element_type=F32)  27.2 us
    unnamed x237, local copies, waits for them, and re-layouts  20.3 us
    psum x1, blocking collectives, local(): gain_sum = lax.psum(gain_total, 'expert')  15.8 us
  transfers between devices with their start and end apart: 120, of which 21 were waited for; matrix products, arithmetic and copies ran while one was open for 8% of the time, Pallas kernels for 0%

profile of v1, /device:TPU:0, one launch (start us, length us, event | category | flops | bytes accessed | tf_op | source)
XLA Modules:
  0.0 492.0 jit_solution(13478809115212741736)
XLA Ops:
  24.5 6.2 %collective-permute-done.4 = bf16[16,2048]{1,0:T(8,128)(2,1)S(1)} collective-permute-done((bf16[16,2048]{1,0:T(8,128)(2,1)S(1)}, bf16[16,2048]{1,0:T(8,128)(2,1)S(1)}, u32[]{:S(2)}, u32[]{:S(2)}) %collective-permute-start.4) | collective-permute-done | bytes 65568 | tf_op jit(solution)/shard_map/ppermute | solution.py:65
  45.5 6.9 %collective-permute-done.11 = bf16[16,2048]{1,0:T(8,128)(2,1)S(1)} collective-permute-done((bf16[16,2048]{1,0:T(8,128)(2,1)S(1)}, bf16[16,2048]{1,0:T(8,128)(2,1)S(1)}, u32[]{:S(2)}, u32[]{:S(2)}) %collective-permute-start.11) | collective-permute-done | bytes 65568 | tf_op jit(solution)/shard_map/ppermute | solution.py:65
  56.2 5.9 %collective-permute-done.14 = bf16[64,2048]{1,0:T(8,128)(2,1)S(1)} collective-permute-done((bf16[64,2048]{1,0:T(8,128)(2,1)S(1)}, bf16[64,2048]{1,0:T(8,128)(2,1)S(1)}, u32[]{:S(2)}, u32[]{:S(2)}) %collective-permute-start.14) | collective-permute-done | bytes 262176 | tf_op jit(solution)/shard_map/ppermute | solution.py:239
  74.3 6.1 %collective-permute-done.19 = bf16[16,2048]{1,0:T(8,128)(2,1)S(1)} collective-permute-done((bf16[16,2048]{1,0:T(8,128)(2,1)S(1)}, bf16[16,2048]{1,0:T(8,128)(2,1)S(1)}, u32[]{:S(2)}, u32[]{:S(2)}) %collective-permute-start.19) | collective-permute-done | bytes 65568 | tf_op jit(solution)/shard_map/ppermute | solution.py:65
  95.2 6.3 %collective-permute-done.26 = bf16[16,2048]{1,0:T(8,128)(2,1)S(1)} collective-permute-done((bf16[16,2048]{1,0:T(8,128)(2,1)S(1)}, bf16[16,2048]{1,0:T(8,128)(2,1)S(1)}, u32[]{:S(2)}, u32[]{:S(2)}) %collective-permute-start.26) | collective-permute-done | bytes 65568 | tf_op jit(solution)/shard_map/ppermute | solution.py:65
  102.4 4.6 collective-permute-start.29
  107.0 5.7 %collective-permute-done.29 = bf16[64,2048]{1,0:T(8,128)(2,1)S(1)} collective-permute-done((bf16[64,2048]{1,0:T(8,128)(2,1)S(1)}, bf16[64,2048]{1,0:T(8,128)(2,1)S(1)}, u32[]{:S(2)}, u32[]{:S(2)}) %collective-permute-start.29) | collective-permute-done | bytes 262176 | tf_op jit(solution)/shard_map/ppermute | solution.py:239
  131.8 5.0 %broadcast_select_fusion = (f32[128,1536]{1,0:T(8,128)}, f32[128,1536]{1,0:T(8,128)S(1)}) fusion(f32[128,1536]{1,0:T(8,128)S(1)} %fusion.252, pred[]{:T(512)S(6)} %eq.37, bf16[128,2048]{1,0:T(8,128)(2,1)} %constant_dynamic-update-slice_fusion.32, bf16[1,1,2048,1536]{3,2,1,0:T(8,128)(2,1)} %param.17), kind=kOutput, calls=%fused_computation.229 | convolution fusion | flops 805502976 | bytes 9175041 | tf_op jit(solution)/shard_map/dot_general | solution.py:20
  147.7 6.2 %collective-permute-done.41 = bf16[16,2048]{1,0:T(8,128)(2,1)S(1)} collective-permute-done((bf16[16,2048]{1,0:T(8,128)(2,1)S(1)}, bf16[16,2048]{1,0:T(8,128)(2,1)S(1)}, u32[]{:S(2)}, u32[]{:S(2)}) %collective-permute-start.41) | collective-permute-done | bytes 65568 | tf_op jit(solution)/shard_map/ppermute | solution.py:65
  174.5 7.2 %conditional.3 = (bf16[128,2048]{1,0:T(8,128)(2,1)S(1)}, bf16[128,128]{1,0:T(8,128)(2,1)}, f32[128,1536]{1,0:T(8,128)}) conditional(s32[]{:T(128)} %convert_element_type.310, (bf16[128,2048]{1,0:T(8,128)(2,1)S(1)}, bf16[2048,1536]{1,0:T(8,128)(2,1)}, bf16[768,2048]{1,0:T(8,128)(2,1)}) %tuple.240, (bf16[128,2048]{1,0:T(8,128)(2,1)}, ...), branch_computations={%region_18.19_spmd, %region_19.21_spmd} | conditional | flops 2015822336 | bytes 34378320
  174.5 4.8 fusion.291
  193.2 6.6 %collective-permute-done.56 = bf16[16,2176]{1,0:T(8,128)(2,1)S(1)} collective-permute-done((bf16[16,2176]{1,0:T(8,128)(2,1)S(1)}, bf16[16,2176]{1,0:T(8,128)(2,1)S(1)}, u32[]{:S(2)}, u32[]{:S(2)}) %collective-permute-start.56) | collective-permute-done | bytes 69664 | tf_op jit(solution)/shard_map/ppermute | solution.py:65
  234.5 5.8 %convolution_convert_fusion.6 = bf16[128,2048]{1,0:T(8,128)(2,1)} fusion(bf16[128,768]{1,0:T(8,128)(2,1)S(1)} %get-tuple-element.156, bf16[128,768]{1,0:T(8,128)(2,1)} %get-tuple-element.157, bf16[1,1,2048,1536]{3,2,1,0:T(8,128)(2,1)} %param.17), kind=kOutput, calls=%fused_computation.29 | convolution fusion | flops 806354944 | bytes 7208960 | tf_op jit(solution)/shard_map/dot_general | solution.py:24
  251.6 6.6 %collective-permute-done.71 = bf16[16,2176]{1,0:T(8,128)(2,1)S(1)} collective-permute-done((bf16[16,2176]{1,0:T(8,128)(2,1)S(1)}, bf16[16,2176]{1,0:T(8,128)(2,1)S(1)}, u32[]{:S(2)}, u32[]{:S(2)}) %collective-permute-start.71) | collective-permute-done | bytes 69664 | tf_op jit(solution)/shard_map/ppermute | solution.py:65
  272.3 6.2 %collective-permute-done.79 = bf16[16,2048]{1,0:T(8,128)(2,1)S(1)} collective-permute-done((bf16[16,2048]{1,0:T(8,128)(2,1)S(1)}, bf16[16,2048]{1,0:T(8,128)(2,1)S(1)}, u32[]{:S(2)}, u32[]{:S(2)}) %collective-permute-start.79) | collective-permute-done | bytes 65568 | tf_op jit(solution)/shard_map/ppermute | solution.py:65
  292.0 6.1 %collective-permute-done.86 = bf16[16,2048]{1,0:T(8,128)(2,1)S(1)} collective-permute-done((bf16[16,2048]{1,0:T(8,128)(2,1)S(1)}, bf16[16,2048]{1,0:T(8,128)(2,1)S(1)}, u32[]{:S(2)}, u32[]{:S(2)}) %collective-permute-start.86) | collective-permute-done | bytes 65568 | tf_op jit(solution)/shard_map/ppermute | solution.py:65
  301.7 40.3 %collective-permute-done.89 = bf16[64,2048]{1,0:T(8,128)(2,1)S(1)} collective-permute-done((bf16[64,2048]{1,0:T(8,128)(2,1)S(1)}, bf16[64,2048]{1,0:T(8,128)(2,1)S(1)}, u32[]{:S(2)}, u32[]{:S(2)}) %collective-permute-start.89) | collective-permute-done | bytes 262176 | tf_op jit(solution)/shard_map/ppermute | solution.py:239
  352.7 5.7 %collective-permute-done.94 = bf16[16,2048]{1,0:T(8,128)(2,1)S(1)} collective-permute-done((bf16[16,2048]{1,0:T(8,128)(2,1)S(1)}, bf16[16,2048]{1,0:T(8,128)(2,1)S(1)}, u32[]{:S(2)}, u32[]{:S(2)}) %collective-permute-start.94) | collective-permute-done | bytes 65568 | tf_op jit(solution)/shard_map/ppermute | solution.py:65
  371.9 6.1 %collective-permute-done.101 = bf16[16,2048]{1,0:T(8,128)(2,1)S(1)} collective-permute-done((bf16[16,2048]{1,0:T(8,128)(2,1)S(1)}, bf16[16,2048]{1,0:T(8,128)(2,1)S(1)}, u32[]{:S(2)}, u32[]{:S(2)}) %collective-permute-start.101) | collective-permute-done | bytes 65568 | tf_op jit(solution)/shard_map/ppermute | solution.py:65
  380.9 10.3 %collective-permute-done.104 = bf16[64,2048]{1,0:T(8,128)(2,1)S(1)} collective-permute-done((bf16[64,2048]{1,0:T(8,128)(2,1)S(1)}, bf16[64,2048]{1,0:T(8,128)(2,1)S(1)}, u32[]{:S(2)}, u32[]{:S(2)}) %collective-permute-start.104) | collective-permute-done | bytes 262176 | tf_op jit(solution)/shard_map/ppermute | solution.py:239
  414.2 4.9 %convolution_convert_fusion = bf16[128,2048]{1,0:T(8,128)(2,1)S(1)} fusion(bf16[128,768]{1,0:T(8,128)(2,1)S(1)} %get-tuple-element.150, bf16[128,768]{1,0:T(8,128)(2,1)S(1)} %get-tuple-element.149, bf16[1,1,2048,1536]{3,2,1,0:T(8,128)(2,1)} %param.17), kind=kOutput, calls=%fused_computation.23 | convolution fusion | flops 806354944 | bytes 7208960 | tf_op jit(solution)/shard_map/dot_general | solution.py:24
  419.4 32.1 %all-reduce.2.cloned.1.call-done = f32[8,2048]{1,0:T(8,128)} async-done(((f32[8,2048]{1,0:T(8,128)}), f32[8,2048]{1,0:T(8,128)}) %all-reduce.2.cloned.1.call-update) | async-done | bytes 65552 | tf_op jit(solution)/shard_map/psum | solution.py:240
  459.8 6.3 %collective-permute-done.116 = bf16[16,2048]{1,0:T(8,128)(2,1)S(1)} collective-permute-done((bf16[16,2048]{1,0:T(8,128)(2,1)S(1)}, bf16[16,2048]{1,0:T(8,128)(2,1)S(1)}, u32[]{:S(2)}, u32[]{:S(2)}) %collective-permute-start.116) | collective-permute-done | bytes 65568 | tf_op jit(solution)/shard_map/ppermute | solution.py:65
  467.0 15.8 %psum.15 = f32[2048]{0:T(1024)S(1)} all-reduce(f32[2048]{0:T(1024)S(1)} %select_add_fusion), channel_id=1, replica_groups=mesh['section'=4,'expert'=8] {'expert'}, use_global_device_ids=true, to_apply=%region_56.57 | all-reduce | flops 2048 | bytes 16384 | tf_op jit(solution)/shard_map/psum | solution.py:241
  (637 shorter events, 264.6 us)
Async XLA Ops:
  7.2 444.3 %all-reduce.2.cloned.1.call-start = ((), (), s32[]{:S(2)}) async-start(), calls=%async_computation | async-start | bytes 131072 | tf_op jit(solution)/shard_map/psum | solution.py:240
  20.3 10.5 %collective-permute-start.4 = (bf16[16,2048]{1,0:T(8,128)(2,1)S(1)}, bf16[16,2048]{1,0:T(8,128)(2,1)S(1)}, u32[]{:S(2)}, u32[]{:S(2)}) collective-permute-start(bf16[16,2048]{1,0:T(8,128)(2,1)S(1)} %get-tuple-element.280), channel_id=1, source_target_pairs={{0,5},{1,4},{2,7},{3,6},{4,1},{5,0},{6,3},{7,2},{8,13},{9,12},{10,... | collective-permute-start | bytes 196616 | tf_op jit(solution)/shard_map/ppermute | solution.py:65
  42.1 10.3 %collective-permute-start.11 = (bf16[16,2048]{1,0:T(8,128)(2,1)S(1)}, bf16[16,2048]{1,0:T(8,128)(2,1)S(1)}, u32[]{:S(2)}, u32[]{:S(2)}) collective-permute-start(bf16[16,2048]{1,0:T(8,128)(2,1)S(1)} %get-tuple-element.272), channel_id=1, source_target_pairs={{0,5},{1,4},{2,7},{3,6},{4,1},{5,0},{6,3},{7,2},{8,13},{9,12},{10,... | collective-permute-start | bytes 196616 | tf_op jit(solution)/shard_map/ppermute | solution.py:65
  42.1 10.3 %collective-permute-start.12 = (bf16[16,2048]{1,0:T(8,128)(2,1)S(1)}, bf16[16,2048]{1,0:T(8,128)(2,1)S(1)}, u32[]{:S(2)}, u32[]{:S(2)}) collective-permute-start(bf16[16,2048]{1,0:T(8,128)(2,1)S(1)} %get-tuple-element.271), channel_id=1, source_target_pairs={{0,6},{1,7},{2,4},{3,5},{4,2},{5,3},{6,0},{7,1},{8,14},{9,15},{10,... | collective-permute-start | bytes 196616 | tf_op jit(solution)/shard_map/ppermute | solution.py:65
  69.8 10.5 %collective-permute-start.19 = (bf16[16,2048]{1,0:T(8,128)(2,1)S(1)}, bf16[16,2048]{1,0:T(8,128)(2,1)S(1)}, u32[]{:S(2)}, u32[]{:S(2)}) collective-permute-start(bf16[16,2048]{1,0:T(8,128)(2,1)S(1)} %get-tuple-element.264), channel_id=1, source_target_pairs={{0,5},{1,4},{2,7},{3,6},{4,1},{5,0},{6,3},{7,2},{8,13},{9,12},{10,... | collective-permute-start | bytes 196616 | tf_op jit(solution)/shard_map/ppermute | solution.py:65
  102.4 10.3 %collective-permute-start.29 = (bf16[64,2048]{1,0:T(8,128)(2,1)S(1)}, bf16[64,2048]{1,0:T(8,128)(2,1)S(1)}, u32[]{:S(2)}, u32[]{:S(2)}) collective-permute-start(bf16[64,2048]{1,0:T(8,128)(2,1)S(1)} %fusion.85), channel_id=1, source_target_pairs={{8,16},{0,8},{9,17},{1,9},{10,18},{2,10},{11,19},{3,11},{12,20},{4... | collective-permute-start | bytes 786440 | tf_op jit(solution)/shard_map/ppermute | solution.py:239
  119.4 10.5 %collective-permute-start.34 = (bf16[16,2048]{1,0:T(8,128)(2,1)S(1)}, bf16[16,2048]{1,0:T(8,128)(2,1)S(1)}, u32[]{:S(2)}, u32[]{:S(2)}) collective-permute-start(bf16[16,2048]{1,0:T(8,128)(2,1)S(1)} %get-tuple-element.248), channel_id=1, source_target_pairs={{0,5},{1,4},{2,7},{3,6},{4,1},{5,0},{6,3},{7,2},{8,13},{9,12},{10,... | collective-permute-start | bytes 196616 | tf_op jit(solution)/shard_map/ppermute | solution.py:65
  143.6 10.4 %collective-permute-start.41 = (bf16[16,2048]{1,0:T(8,128)(2,1)S(1)}, bf16[16,2048]{1,0:T(8,128)(2,1)S(1)}, u32[]{:S(2)}, u32[]{:S(2)}) collective-permute-start(bf16[16,2048]{1,0:T(8,128)(2,1)S(1)} %get-tuple-element.240), channel_id=1, source_target_pairs={{0,5},{1,4},{2,7},{3,6},{4,1},{5,0},{6,3},{7,2},{8,13},{9,12},{10,... | collective-permute-start | bytes 196616 | tf_op jit(solution)/shard_map/ppermute | solution.py:65
  157.9 10.6 %collective-permute-start.46 = (bf16[16,2048]{1,0:T(8,128)(2,1)}, bf16[16,2048]{1,0:T(8,128)(2,1)}, u32[]{:S(2)}, u32[]{:S(2)}) collective-permute-start(bf16[16,2048]{1,0:T(8,128)(2,1)} %get-tuple-element.235), channel_id=1, source_target_pairs={{0,2},{1,3},{2,0},{3,1},{4,6},{5,7},{6,4},{7,5},{8,10},{9,11},{10,... | collective-permute-start | bytes 196616 | tf_op jit(solution)/shard_map/ppermute | solution.py:65
  161.3 10.8 %collective-permute-start.48 = (bf16[16,2048]{1,0:T(8,128)(2,1)}, bf16[16,2048]{1,0:T(8,128)(2,1)}, u32[]{:S(2)}, u32[]{:S(2)}) collective-permute-start(bf16[16,2048]{1,0:T(8,128)(2,1)} %get-tuple-element.233), channel_id=1, source_target_pairs={{0,4},{1,5},{2,6},{3,7},{4,0},{5,1},{6,2},{7,3},{8,12},{9,13},{10,... | collective-permute-start | bytes 196616 | tf_op jit(solution)/shard_map/ppermute | solution.py:65
  189.0 10.9 %collective-permute-start.56 = (bf16[16,2176]{1,0:T(8,128)(2,1)S(1)}, bf16[16,2176]{1,0:T(8,128)(2,1)S(1)}, u32[]{:S(2)}, u32[]{:S(2)}) collective-permute-start(bf16[16,2176]{1,0:T(8,128)(2,1)S(1)} %get-tuple-element.172), channel_id=1, source_target_pairs={{0,5},{1,4},{2,7},{3,6},{4,1},{5,0},{6,3},{7,2},{8,13},{9,12},{10,... | collective-permute-start | bytes 208904 | tf_op jit(solution)/shard_map/ppermute | solution.py:65
  189.2 10.7 %collective-permute-start.57 = (bf16[16,2176]{1,0:T(8,128)(2,1)S(1)}, bf16[16,2176]{1,0:T(8,128)(2,1)S(1)}, u32[]{:S(2)}, u32[]{:S(2)}) collective-permute-start(bf16[16,2176]{1,0:T(8,128)(2,1)S(1)} %get-tuple-element.173), channel_id=1, source_target_pairs={{0,6},{1,7},{2,4},{3,5},{4,2},{5,3},{6,0},{7,1},{8,14},{9,15},{10,... | collective-permute-start | bytes 208904 | tf_op jit(solution)/shard_map/ppermute | solution.py:65
  216.7 10.4 %collective-permute-start.64 = (bf16[16,2048]{1,0:T(8,128)(2,1)S(1)}, bf16[16,2048]{1,0:T(8,128)(2,1)S(1)}, u32[]{:S(2)}, u32[]{:S(2)}) collective-permute-start(bf16[16,2048]{1,0:T(8,128)(2,1)S(1)} %get-tuple-element.224), channel_id=1, source_target_pairs={{0,5},{1,4},{2,7},{3,6},{4,1},{5,0},{6,3},{7,2},{8,13},{9,12},{10,... | collective-permute-start | bytes 196616 | tf_op jit(solution)/shard_map/ppermute | solution.py:65
  247.4 10.9 %collective-permute-start.71 = (bf16[16,2176]{1,0:T(8,128)(2,1)S(1)}, bf16[16,2176]{1,0:T(8,128)(2,1)S(1)}, u32[]{:S(2)}, u32[]{:S(2)}) collective-permute-start(bf16[16,2176]{1,0:T(8,128)(2,1)S(1)} %get-tuple-element.160), channel_id=1, source_target_pairs={{0,5},{1,4},{2,7},{3,6},{4,1},{5,0},{6,3},{7,2},{8,13},{9,12},{10,... | collective-permute-start | bytes 208904 | tf_op jit(solution)/shard_map/ppermute | solution.py:65
  247.6 10.6 %collective-permute-start.72 = (bf16[16,2176]{1,0:T(8,128)(2,1)S(1)}, bf16[16,2176]{1,0:T(8,128)(2,1)S(1)}, u32[]{:S(2)}, u32[]{:S(2)}) collective-permute-start(bf16[16,2176]{1,0:T(8,128)(2,1)S(1)} %get-tuple-element.159), channel_id=1, source_target_pairs={{0,6},{1,7},{2,4},{3,5},{4,2},{5,3},{6,0},{7,1},{8,14},{9,15},{10,... | collective-permute-start | bytes 208904 | tf_op jit(solution)/shard_map/ppermute | solution.py:65
  268.2 10.3 %collective-permute-start.79 = (bf16[16,2048]{1,0:T(8,128)(2,1)S(1)}, bf16[16,2048]{1,0:T(8,128)(2,1)S(1)}, u32[]{:S(2)}, u32[]{:S(2)}) collective-permute-start(bf16[16,2048]{1,0:T(8,128)(2,1)S(1)} %get-tuple-element.216), channel_id=1, source_target_pairs={{0,5},{1,4},{2,7},{3,6},{4,1},{5,0},{6,3},{7,2},{8,13},{9,12},{10,... | collective-permute-start | bytes 196616 | tf_op jit(solution)/shard_map/ppermute | solution.py:65
  287.7 10.5 %collective-permute-start.86 = (bf16[16,2048]{1,0:T(8,128)(2,1)S(1)}, bf16[16,2048]{1,0:T(8,128)(2,1)S(1)}, u32[]{:S(2)}, u32[]{:S(2)}) collective-permute-start(bf16[16,2048]{1,0:T(8,128)(2,1)S(1)} %get-tuple-element.208), channel_id=1, source_target_pairs={{0,5},{1,4},{2,7},{3,6},{4,1},{5,0},{6,3},{7,2},{8,13},{9,12},{10,... | collective-permute-start | bytes 196616 | tf_op jit(solution)/shard_map/ppermute | solution.py:65
  299.7 42.3 %collective-permute-start.89 = (bf16[64,2048]{1,0:T(8,128)(2,1)S(1)}, bf16[64,2048]{1,0:T(8,128)(2,1)S(1)}, u32[]{:S(2)}, u32[]{:S(2)}) collective-permute-start(bf16[64,2048]{1,0:T(8,128)(2,1)S(1)} %fusion.61), channel_id=1, source_target_pairs={{8,0},{16,8},{9,1},{17,9},{10,2},{18,10},{11,3},{19,11},{12,4},{20... | collective-permute-start | bytes 786440 | tf_op jit(solution)/shard_map/ppermute | solution.py:239
  348.1 10.4 %collective-permute-start.94 = (bf16[16,2048]{1,0:T(8,128)(2,1)S(1)}, bf16[16,2048]{1,0:T(8,128)(2,1)S(1)}, u32[]{:S(2)}, u32[]{:S(2)}) collective-permute-start(bf16[16,2048]{1,0:T(8,128)(2,1)S(1)} %get-tuple-element.200), channel_id=1, source_target_pairs={{0,5},{1,4},{2,7},{3,6},{4,1},{5,0},{6,3},{7,2},{8,13},{9,12},{10,... | collective-permute-start | bytes 196616 | tf_op jit(solution)/shard_map/ppermute | solution.py:65
  367.6 10.4 %collective-permute-start.101 = (bf16[16,2048]{1,0:T(8,128)(2,1)S(1)}, bf16[16,2048]{1,0:T(8,128)(2,1)S(1)}, u32[]{:S(2)}, u32[]{:S(2)}) collective-permute-start(bf16[16,2048]{1,0:T(8,128)(2,1)S(1)} %get-tuple-element.192), channel_id=1, source_target_pairs={{0,5},{1,4},{2,7},{3,6},{4,1},{5,0},{6,3},{7,2},{8,13},{9,12},{10,... | collective-permute-start | bytes 196616 | tf_op jit(solution)/shard_map/ppermute | solution.py:65
  379.0 12.3 %collective-permute-start.104 = (bf16[64,2048]{1,0:T(8,128)(2,1)S(1)}, bf16[64,2048]{1,0:T(8,128)(2,1)S(1)}, u32[]{:S(2)}, u32[]{:S(2)}) collective-permute-start(bf16[64,2048]{1,0:T(8,128)(2,1)S(1)} %fusion.69), channel_id=1, source_target_pairs={{8,0},{9,1},{10,2},{11,3},{12,4},{13,5},{14,6},{15,7}} | collective-permute-start | bytes 786440 | tf_op jit(solution)/shard_map/ppermute | solution.py:239
  398.3 10.6 %collective-permute-start.109 = (bf16[16,2048]{1,0:T(8,128)(2,1)S(1)}, bf16[16,2048]{1,0:T(8,128)(2,1)S(1)}, u32[]{:S(2)}, u32[]{:S(2)}) collective-permute-start(bf16[16,2048]{1,0:T(8,128)(2,1)S(1)} %get-tuple-element.184), channel_id=1, source_target_pairs={{0,5},{1,4},{2,7},{3,6},{4,1},{5,0},{6,3},{7,2},{8,13},{9,12},{10,... | collective-permute-start | bytes 196616 | tf_op jit(solution)/shard_map/ppermute | solution.py:65
  419.2 38.1 %collective-permute-start.112 = (bf16[16,2048]{1,0:T(8,128)(2,1)S(1)}, bf16[16,2048]{1,0:T(8,128)(2,1)S(1)}, u32[]{:S(2)}, u32[]{:S(2)}) collective-permute-start(bf16[16,2048]{1,0:T(8,128)(2,1)S(1)} %get-tuple-element.180), channel_id=1, source_target_pairs={{0,1},{1,0},{2,3},{3,2},{4,5},{5,4},{6,7},{7,6},{8,9},{9,8},{10,11... | collective-permute-start | bytes 196616 | tf_op jit(solution)/shard_map/ppermute | solution.py:65
  454.9 11.2 %collective-permute-start.116 = (bf16[16,2048]{1,0:T(8,128)(2,1)S(1)}, bf16[16,2048]{1,0:T(8,128)(2,1)S(1)}, u32[]{:S(2)}, u32[]{:S(2)}) collective-permute-start(bf16[16,2048]{1,0:T(8,128)(2,1)S(1)} %get-tuple-element.176), channel_id=1, source_target_pairs={{0,5},{1,4},{2,7},{3,6},{4,1},{5,0},{6,3},{7,2},{8,13},{9,12},{10,... | collective-permute-start | bytes 196616 | tf_op jit(solution)/shard_map/ppermute | solution.py:65
  (167 other events, 1916.8 us)
Sparse Core Ops, SparseCore 0:
  399.6 51.8 all-reduce.1
